TPU v7x, 32 devices: a whole 2x2x4 slice. The times are simulated.
32 devices in a mesh: expert: 4 (over x, core), context: 2 (over y), dp: 4 (over z).
Axes of the slice: x: 2, y: 2, z: 4, core: 2. Of those that a mesh axis runs over, the one named last changes fastest.
Arguments:
- tokens: bfloat16 [16, 512, 1024], P(('expert', 'dp'), 'context'), may hold values from -6 to 6
- span_order: int32 [4], replicated, may hold values from 0 to 3, each once
- routes: int32 [16, 512, 8], P(('expert', 'dp'), 'context'), may hold values from 0 to 15, all different within a row; in each aligned block of 256 rows (0 to 255, 256 to 511, ..., all dimensions but the last counted through in order) at most 160 rows name the same one
- norm_attn: bfloat16 [1024], replicated, may hold values from 0.5 to 1.5
- w_query: bfloat16 [1024, 1024], replicated, may hold values from -0.1875 to 0.1875
- w_key: bfloat16 [1024, 512], replicated, may hold values from -0.1875 to 0.1875
- w_value: bfloat16 [1024, 512], replicated, may hold values from -0.1875 to 0.1875
- w_out: bfloat16 [1024, 1024], replicated, may hold values from -1.5 to 1.5
- norm_moe: bfloat16 [1024], replicated, may hold values from 0.5 to 1.5
- w_router: bfloat16 [1024, 16], replicated, may hold values from -0.09375 to 0.09375
- w_gate: bfloat16 [16, 1024, 512], P('expert'), may hold values from -0.1875 to 0.1875
- w_up: bfloat16 [16, 1024, 512], P('expert'), may hold values from -0.1875 to 0.1875
- w_down: bfloat16 [16, 512, 1024], P('expert'), may hold values from -1 to 1
- cotangent: bfloat16 [16, 512, 1024], P(('expert', 'dp'), 'context'), may hold values from -6 to 6
Outputs:
- outputs: bfloat16 [16, 512, 1024], P(('expert', 'dp'), 'context')
- grad_tokens: bfloat16 [16, 512, 1024], P(('expert', 'dp'), 'context')
- grad_norm_attn: float32 [1024], replicated
- grad_query: float32 [1024, 1024], replicated
- grad_key: float32 [1024, 512], replicated
- grad_value: float32 [1024, 512], replicated
- grad_out: float32 [1024, 1024], replicated
- grad_norm_moe: float32 [1024], replicated
- grad_router: float32 [1024, 16], replicated
- grad_gate: float32 [16, 1024, 512], P('expert')
- grad_up: float32 [16, 1024, 512], P('expert')
- grad_down: float32 [16, 512, 1024], P('expert')
Inputs may be any that keep to these rules, and one draw needn't show every extreme that they name: span_order is a permutation; stored block j of every sequence holds the tokens at positions span_order[j] * 128 to span_order[j] * 128 + 127. `routes`: each token names 8 different experts. Within the rows of one device (aligned blocks of 256 rows, in order), no expert is named by more than 160 rows, a bound that some block reaches.
All inputs are finite; a program needn't handle non-finite values.
Results may differ from a plain program's by a relative error of at most 0.017.
Values may be sent and summed in bfloat16 or wider, within the bound.
A program may use at most 192 MiB of HBM per device.

v0:
```python
import math
import jax
import jax.numpy as jnp
from jax import lax
from jax.sharding import PartitionSpec as P

H = 16
KV = 8
HD = 64
EXPERTS = 16
SPAN = 128
EPSILON = 1e-06
ROPE_BASE = 10000.0
MASKED = -1e30
F32 = jnp.float32
BF16 = jnp.bfloat16


def rope_tables(positions):
    half_dim = HD // 2
    frequency = ROPE_BASE ** (-(jnp.arange(half_dim, dtype=F32) * 2.0) / HD)
    angles = positions.astype(F32)[:, None] * frequency[None, :]
    return (jnp.cos(angles), jnp.sin(angles))


def rotate(tensor, cos_table, sin_table):
    half_dim = tensor.shape[-1] // 2
    front = tensor[..., :half_dim]
    back = tensor[..., half_dim:]
    cos_wide = cos_table[:, None, :]
    sin_wide = sin_table[:, None, :]
    return jnp.concatenate(
        [front * cos_wide - back * sin_wide, back * cos_wide + front * sin_wide], axis=-1
    )


def positions_of(row_index, span_order):
    block_ids = row_index // SPAN
    picked = jnp.where(
        block_ids[:, None] == jnp.arange(span_order.shape[0], dtype=jnp.int32)[None, :],
        span_order[None, :],
        0,
    )
    return jnp.sum(picked, axis=1, dtype=jnp.int32) * SPAN + row_index % SPAN


def norm_back(grad_normed, normed, inv_root):
    return inv_root * (
        grad_normed - normed * jnp.mean(grad_normed * normed, axis=-1, keepdims=True)
    )


def dot(a, b):
    return jnp.dot(a, b, preferred_element_type=F32)


def dot_t(a, b):
    return lax.dot_general(a, b, (((1,), (1,)), ((), ())), preferred_element_type=F32)


def t_dot(a, b):
    return lax.dot_general(a, b, (((0,), (0,)), ((), ())), preferred_element_type=F32)


def body(
    tokens,
    span_order,
    routes,
    norm_attn,
    w_query,
    w_key,
    w_value,
    w_out,
    norm_moe,
    w_router,
    w_gate,
    w_up,
    w_down,
    cotangent,
):
    tok_rows = tokens.shape[1]
    width = tokens.shape[2]
    seq_rows = tok_rows * lax.axis_size("context")
    groups = H // KV
    score_scale = 1.0 / math.sqrt(HD)
    local_experts = w_gate.shape[0]
    ff = w_gate.shape[2]
    dy_all = lax.all_gather(cotangent[0], "expert", axis=0, tiled=True)
    routes_all = lax.all_gather(routes[0], "expert", axis=0, tiled=True)
    local_index = lax.axis_index("context") * tok_rows + jnp.arange(tok_rows, dtype=jnp.int32)
    pos_query = positions_of(local_index, span_order)
    pos_keys = positions_of(jnp.arange(seq_rows, dtype=jnp.int32), span_order)
    cos_table, sin_table = rope_tables(pos_query)
    allowed = pos_keys[None, :] <= pos_query[:, None]
    inputs = tokens[0].astype(F32)
    inv_one = lax.rsqrt(jnp.mean(inputs * inputs, axis=-1, keepdims=True) + EPSILON)
    normed_one = inputs * inv_one
    gain_one = norm_attn.astype(F32)
    h_one = (normed_one * gain_one).astype(BF16)
    key_pre = dot(h_one, w_key).reshape(tok_rows, KV, HD)
    keys_local = rotate(key_pre, cos_table, sin_table).astype(BF16).reshape(tok_rows, KV * HD)
    values_local = dot(h_one, w_value).astype(BF16)
    kv_all = lax.all_gather(
        jnp.concatenate([keys_local, values_local], axis=1), "context", axis=0, tiled=True
    )
    query_pre = dot(h_one, w_query).reshape(tok_rows, H, HD)
    queries = rotate(query_pre, cos_table, sin_table).astype(BF16).reshape(tok_rows, KV, groups, HD)
    keys_all = kv_all[:, : KV * HD].reshape(seq_rows, KV, HD)
    values_all = kv_all[:, KV * HD :].reshape(seq_rows, KV, HD)
    scores = (
        jnp.einsum("qkgd,skd->kgqs", queries, keys_all, preferred_element_type=F32) * score_scale
    )
    masked = jnp.where(allowed, scores, MASKED)
    top_score = jnp.max(masked, axis=-1, keepdims=True)
    exp_scores = jnp.exp(masked - top_score)
    total_exp = jnp.sum(exp_scores, axis=-1, keepdims=True)
    attn_probs = exp_scores / total_exp
    probs_rounded = attn_probs.astype(BF16)
    mixed_heads = jnp.einsum(
        "kgqs,skd->qkgd", probs_rounded, values_all, preferred_element_type=F32
    )
    mixed_heads = mixed_heads.reshape(tok_rows, H * HD).astype(BF16)
    y_one = inputs + dot(mixed_heads, w_out)
    inv_two = lax.rsqrt(jnp.mean(y_one * y_one, axis=-1, keepdims=True) + EPSILON)
    normed_two = y_one * inv_two
    gain_two = norm_moe.astype(F32)
    h_two = (normed_two * gain_two).astype(BF16)
    h_all = lax.all_gather(h_two, "expert", axis=0, tiled=True)
    experts = jnp.arange(EXPERTS, dtype=jnp.int32)
    chosen = jnp.any(routes_all[:, :, None] == experts[None, None, :], axis=1)
    logits = jnp.where(chosen, dot(h_all, w_router), MASKED)
    weights = jnp.where(chosen, jnp.exp(logits - jnp.max(logits, axis=-1, keepdims=True)), 0.0)
    weights = weights / jnp.sum(weights, axis=-1, keepdims=True)
    me = lax.axis_index("expert")
    mine = lax.dynamic_slice_in_dim(weights, me * local_experts, local_experts, axis=1)
    partial_y = None
    partial_h = None
    dots = []
    g_gate, g_up, g_down = ([], [], [])
    for e in range(local_experts):
        weight = mine[:, e : e + 1]
        gate_pre = dot(h_all, w_gate[e])
        upward = dot(h_all, w_up[e])
        back = dot_t(dy_all, w_down[e])
        sigmoid_gate = jax.nn.sigmoid(gate_pre)
        silu_gate = gate_pre * sigmoid_gate
        hidden = silu_gate * upward
        hidden_w = (hidden * weight).astype(BF16)
        dots.append(jnp.sum(hidden * back, axis=-1, keepdims=True))
        grad_hidden = back * weight
        grad_gate_pre = (
            grad_hidden * upward * sigmoid_gate * (1.0 + gate_pre * (1.0 - sigmoid_gate))
        ).astype(BF16)
        grad_up_pre = (grad_hidden * silu_gate).astype(BF16)
        add_y = dot(hidden_w, w_down[e])
        add_h = dot_t(grad_gate_pre, w_gate[e]) + dot_t(grad_up_pre, w_up[e])
        partial_y = add_y if partial_y is None else partial_y + add_y
        partial_h = add_h if partial_h is None else partial_h + add_h
        g_down.append(t_dot(hidden_w, dy_all).astype(BF16))
        g_gate.append(t_dot(h_all, grad_gate_pre).astype(BF16))
        g_up.append(t_dot(h_all, grad_up_pre).astype(BF16))
    d_weights = jnp.concatenate(dots, axis=1)
    d_wide = lax.dynamic_update_slice_in_dim(
        jnp.zeros((d_weights.shape[0], EXPERTS), F32), d_weights, me * local_experts, axis=1
    )
    d_high = lax.reduce_precision(d_wide, 8, 7)
    packed = jnp.concatenate(
        [
            partial_h.astype(BF16),
            d_high.astype(BF16),
            (d_wide - d_high).astype(BF16),
            jnp.zeros((d_wide.shape[0], 128 - 2 * EXPERTS), BF16),
        ],
        axis=1,
    )
    home = lax.psum_scatter(packed, "expert", scatter_dimension=0, tiled=True).astype(F32)
    y_two = lax.psum_scatter(
        partial_y.astype(BF16), "expert", scatter_dimension=0, tiled=True
    ).astype(F32)
    total_gate, total_up, total_down = (
        lax.psum(jnp.stack(g), ("context", "dp")).astype(F32) for g in (g_gate, g_up, g_down)
    )
    outputs = (y_one + y_two).astype(BF16)[None]
    grad_final = cotangent[0].astype(F32)
    grad_weights = home[:, width : width + EXPERTS] + home[:, width + EXPERTS : width + 2 * EXPERTS]
    own = lax.dynamic_slice_in_dim(weights, me * tok_rows, tok_rows, axis=0)
    grad_logits = (
        own * (grad_weights - jnp.sum(own * grad_weights, axis=-1, keepdims=True))
    ).astype(BF16)
    grad_router_w = t_dot(h_two, grad_logits)
    grad_h_two = home[:, :width] + dot_t(grad_logits, w_router)
    grad_gain_two = jnp.sum(grad_h_two * normed_two, axis=0)
    grad_y_one = grad_final + norm_back(grad_h_two * gain_two, normed_two, inv_two)
    grad_attn = grad_y_one.astype(BF16)
    grad_out_w = t_dot(mixed_heads, grad_attn)
    grad_mixed = dot_t(grad_attn, w_out).astype(BF16).reshape(tok_rows, KV, groups, HD)
    grad_probs = jnp.einsum("qkgd,skd->kgqs", grad_mixed, values_all, preferred_element_type=F32)
    grad_values = jnp.einsum(
        "kgqs,qkgd->skd", probs_rounded, grad_mixed, preferred_element_type=F32
    )
    row_dots = jnp.sum(attn_probs * grad_probs, axis=-1, keepdims=True)
    grad_scores = (attn_probs * (grad_probs - row_dots)).astype(BF16)
    grad_keys = (
        jnp.einsum("kgqs,qkgd->skd", grad_scores, queries, preferred_element_type=F32) * score_scale
    )
    grad_kv = lax.psum_scatter(
        jnp.concatenate(
            [grad_keys.reshape(seq_rows, KV * HD), grad_values.reshape(seq_rows, KV * HD)], axis=1
        ).astype(BF16),
        "context",
        scatter_dimension=0,
        tiled=True,
    ).astype(F32)
    grad_queries = (
        jnp.einsum("kgqs,skd->qkgd", grad_scores, keys_all, preferred_element_type=F32)
        * score_scale
    )
    grad_q_pre = (
        rotate(grad_queries.reshape(tok_rows, H, HD), cos_table, -sin_table)
        .reshape(tok_rows, H * HD)
        .astype(BF16)
    )
    grad_k_pre = (
        rotate(grad_kv[:, : KV * HD].reshape(tok_rows, KV, HD), cos_table, -sin_table)
        .reshape(tok_rows, KV * HD)
        .astype(BF16)
    )
    grad_v_pre = grad_kv[:, KV * HD :].astype(BF16)
    grad_query_w = t_dot(h_one, grad_q_pre)
    grad_key_w = t_dot(h_one, grad_k_pre)
    grad_value_w = t_dot(h_one, grad_v_pre)
    grad_h_one = dot_t(grad_q_pre, w_query) + dot_t(grad_k_pre, w_key) + dot_t(grad_v_pre, w_value)
    grad_gain_one = jnp.sum(grad_h_one * normed_one, axis=0)
    grad_inputs = grad_y_one + norm_back(grad_h_one * gain_one, normed_one, inv_one)
    grad_tokens = grad_inputs.astype(BF16)[None]
    everywhere = ("expert", "context", "dp")
    total_o = lax.psum(grad_out_w.astype(BF16), everywhere).astype(F32)
    total_q, total_k, total_v = (
        t.astype(F32)
        for t in lax.psum(
            tuple((g.astype(BF16) for g in (grad_query_w, grad_key_w, grad_value_w))), everywhere
        )
    )
    total_g1, total_g2, total_r = lax.psum(
        (grad_gain_one, grad_gain_two, grad_router_w), everywhere
    )
    return (
        outputs,
        grad_tokens,
        total_g1,
        total_q,
        total_k,
        total_v,
        total_o,
        total_g2,
        total_r,
        total_gate,
        total_up,
        total_down,
    )


def solution(mesh):
    in_specs = (
        P(("expert", "dp"), "context", None),
        P(),
        P(("expert", "dp"), "context", None),
        P(),
        P(),
        P(),
        P(),
        P(),
        P(),
        P(),
        P("expert", None, None),
        P("expert", None, None),
        P("expert", None, None),
        P(("expert", "dp"), "context", None),
    )
    out_specs = (
        P(("expert", "dp"), "context", None),
        P(("expert", "dp"), "context", None),
        P(),
        P(),
        P(),
        P(),
        P(),
        P(),
        P(),
        P("expert", None, None),
        P("expert", None, None),
        P("expert", None, None),
    )
    return jax.shard_map(body, mesh=mesh, in_specs=in_specs, out_specs=out_specs, check_vma=False)
```

profile of v0, /device:TPU:1, one launch (start us, length us, event | category | flops | bytes accessed | tf_op | source)
XLA Modules:
  0.0 959.9 jit_solution(15199929937461508150)
XLA Ops:
  9.5 2.3 copy.117
  11.8 2.8 convolution_convert_fusion.13
  16.4 1.8 pad_maximum_fusion.4
  19.1 3.9 copy.122
  23.0 2.4 fusion.161
  27.2 14.6 %all-gather.6.cloned.1.call-done = bf16[512,1024]{1,0:T(8,128)(2,1)} async-done(((bf16[256,1024]{1,0:T(8,128)(2,1)}), bf16[512,1024]{1,0:T(8,128)(2,1)}) %all-gather.6.cloned.1.call-update) | async-done | bytes 1048592 | tf_op jit(solution)/shard_map/all_gather | solution.py:103
  41.8 2.1 fusion.202
  46.1 8.0 fusion.203
  54.1 4.3 fusion.74
  61.6 6.1 all-gather
  67.9 4.6 fusion.16
  72.5 2.6 fusion.18
  75.1 2.6 fusion.20
  77.7 2.6 fusion.22
  80.3 11.1 %all-gather.8.cloned.1.call-done = bf16[1024,1024]{0,1:T(8,128)(2,1)} async-done(((bf16[256,1024]{0,1:T(8,128)(2,1)}), bf16[1024,1024]{0,1:T(8,128)(2,1)}) %all-gather.8.cloned.1.call-update) | async-done | bytes 2097168 | tf_op jit(solution)/shard_map/all_gather | solution.py:128
  91.4 2.1 fusion.204
  94.3 2.7 fusion.94
  102.5 3.8 multiply_convert_fusion.1
  106.3 2.6 multiply_convert_fusion.3
  109.0 3.5 multiply_convert_fusion.5
  112.5 3.5 multiply_convert_fusion.7
  120.6 3.3 fusion.118
  123.9 3.3 fusion.114
  127.2 3.5 fusion.129
  130.7 3.3 fusion.125
  134.0 9.2 add_convert_fusion
  143.2 2.8 maximum_maximum_fusion
  146.1 2.7 fusion.101
  151.6 3.1 add_convert_fusion.1
  156.7 4.3 fusion.47
  161.0 2.3 fusion.46
  163.3 2.3 fusion.45
  165.6 2.3 fusion.44
  167.9 11.0 %reduce-scatter.6.cloned.1.call-done = bf16[256,1152]{0,1:T(8,128)(2,1)} async-done(((bf16[1024,1152]{0,1:T(8,128)(2,1)}), bf16[256,1152]{0,1:T(8,128)(2,1)}) %reduce-scatter.6.cloned.1.call-update) | async-done | bytes 589840 | tf_op jit(solution)/shard_map/reduce_scatter | solution.py:176
  182.5 30.9 %reduce-scatter.4.cloned.1.call-done = bf16[256,1024]{0,1:T(8,128)(2,1)} async-done(((bf16[1024,1024]{0,1:T(8,128)(2,1)}), bf16[256,1024]{0,1:T(8,128)(2,1)}) %reduce-scatter.4.cloned.1.call-update) | async-done | bytes 524304 | tf_op jit(solution)/shard_map/reduce_scatter | solution.py:177
  213.4 2.7 convert_add_fusion
  218.9 4.9 fusion.1
  223.8 4.8 fusion.78
  228.6 4.5 fusion.3
  236.8 4.0 fusion.51
  240.8 2.4 fusion.50
  245.6 2.1 convolution_convert_fusion.1
  247.7 2.1 convolution_convert_fusion
  249.7 7.0 reduce-scatter.8.cloned.1.call-done
  257.9 1.5 convolution_convert_fusion.11
  259.4 1.5 convolution_convert_fusion.10
  260.9 3.3 fusion.49
  271.4 2.4 pad_maximum_fusion.2
  275.8 3.8 pad_maximum_fusion
  279.7 2.1 copy.139
  281.8 1.6 fusion.205
  283.4 3.4 fusion.206
  286.9 2.1 convolution_add_fusion.2
  291.6 39.5 %all-reduce = (f32[1024]{0:T(1024)}, f32[1024]{0:T(1024)}) all-reduce(f32[1024]{0:T(1024)S(1)} %get-tuple-element.26, f32[1024]{0:T(1024)S(1)} %get-tuple-element.24), channel_id=1, replica_groups=mesh['expert'=4,'context'=2,'dp'=4] {'expert','context','dp'}, use_global_device_ids=true, to_apply=%region_21.22 | all-reduce | flops 2048 | bytes 16384 | tf_op jit(solution)/shard_map/psum | solution.py:244
  331.1 90.1 %all-reduce.9.cloned.1.call-done = (bf16[1024,1024]{1,0:T(8,128)(2,1)}, bf16[1024,512]{1,0:T(8,128)(2,1)}, bf16[1024,512]{1,0:T(8,128)(2,1)}, bf16[1024,1024]{1,0:T(8,128)(2,1)}) async-done(((bf16[1024,1024]{1,0:T(8,128)(2,1)}, bf16[1024,512]{1,0:T(8,128)(2,1)}, bf16[1024,512]{1,0:T(8,128)(2,1)}, bf16[1024,1024]{1,0:T(8,128)(2,1)}), (bf16[1024,1024]{1,0:T(8,128)(2,1)}, bf16[1024,512]{1,0:T(8,128)(2,1)}, ...) | async-done | bytes 6291472 | tf_op jit(solution)/shard_map/psum | solution.py:240
  421.2 4.2 convert_element_type.280
  425.3 1.6 convert_element_type.282
  426.9 1.6 convert_element_type.284
  429.3 2.5 convert_element_type.286
  431.8 394.5 %all-reduce.11.cloned.1.call-done = (bf16[4,1024,512]{2,1,0:T(8,128)(2,1)}, bf16[4,1024,512]{2,1,0:T(8,128)(2,1)}, bf16[4,512,1024]{2,1,0:T(8,128)(2,1)}) async-done(((bf16[4,1024,512]{2,1,0:T(8,128)(2,1)}, bf16[4,1024,512]{2,1,0:T(8,128)(2,1)}, bf16[4,512,1024]{2,1,0:T(8,128)(2,1)}), (bf16[4,1024,512]{2,1,0:T(8,128)(2,1)}, bf16[4,1024,512]{2,1,0:T(8,128)(2,1)}, ...) | async-done | bytes 12582928 | tf_op jit(solution)/shard_map/psum | solution.py:181
  826.2 6.9 convert_element_type.291
  833.1 4.6 convert_element_type.296
  837.7 4.4 convert_element_type.301
  842.2 109.5 %all-reduce.7.cloned.1.call-done = f32[1024,16]{0,1:T(8,128)} async-done(((f32[1024,16]{0,1:T(8,128)}), f32[1024,16]{0,1:T(8,128)}) %all-reduce.7.cloned.1.call-update) | async-done | bytes 65552 | tf_op jit(solution)/shard_map/psum | solution.py:244
  (264 shorter events, 55.0 us)
Async XLA Ops:
  7.2 51.3 %copy-start = (bf16[1024,1024]{1,0:T(8,128)(2,1)S(1)}, bf16[1024,1024]{1,0:T(8,128)(2,1)}, u32[]{:S(2)}) copy-start(bf16[1024,1024]{1,0:T(8,128)(2,1)} %param.21) | copy-start | bytes 6291460
  7.2 34.6 %all-gather.6.cloned.1.call-start = ((), (), s32[]{:S(2)}) async-start(), calls=%async_computation.3 | async-start | bytes 1572864 | tf_op jit(solution)/shard_map/all_gather | solution.py:103
  8.6 49.8 %copy-start.3 = (bf16[1,256,1024]{1,2,0:T(8,128)(2,1)}, bf16[1,256,1024]{1,2,0:T(8,128)(2,1)S(1)}, u32[]{:S(2)}) copy-start(bf16[1,256,1024]{1,2,0:T(8,128)(2,1)S(1)} %copy.116) | copy-start | bytes 1572868
  9.4 13.6 %copy-start.62 = (f32[1024]{0:T(1024)}, f32[1024]{0:T(1024)S(1)}, u32[]{:S(2)}) copy-start(f32[1024]{0:T(1024)S(1)} %convert_element_type.237) | copy-start | bytes 12292
  9.5 13.5 %copy-start.64 = (f32[256]{0:T(256)}, f32[256]{0:T(256)S(1)}, u32[]{:S(2)}) copy-start(f32[256]{0:T(256)S(1)} %add_rsqrt_fusion.1) | copy-start | bytes 3076
  11.8 2.8 copy-start.46
  11.8 3.4 copy-start.69
  16.1 10.2 %copy-start.47 = (f32[256,32]{0,1:T(8,128)}, f32[256,32]{0,1:T(8,128)S(1)}, u32[]{:S(2)}) copy-start(f32[256,32]{0,1:T(8,128)S(1)} %get-tuple-element.75) | copy-start | bytes 98308
  18.2 49.6 %all-gather.10.cloned.1.call-start = ((), (), s32[]{:S(2)}) async-start(), calls=%async_computation.9 | async-start | bytes 2621440 | tf_op jit(solution)/shard_map/all_gather | solution.py:88
  18.9 72.4 %all-gather.8.cloned.1.call-start = ((), (), s32[]{:S(2)}) async-start(), calls=%async_computation.4 | async-start | bytes 2621440 | tf_op jit(solution)/shard_map/all_gather | solution.py:128
  23.0 2.4 copy-start.68
  27.2 18.9 %copy-start.43 = (bf16[256,16,32]{0,2,1:T(8,128)(2,1)}, bf16[256,16,32]{0,2,1:T(8,128)(2,1)S(1)}, u32[]{:S(2)}) copy-start(bf16[256,16,32]{0,2,1:T(8,128)(2,1)S(1)} %get-tuple-element.57) | copy-start | bytes 786436
  27.2 18.9 %copy-start.61 = (pred[256,512]{0,1:T(8,128)(4,1)S(1)}, pred[256,512]{0,1:T(8,128)(4,1)}, u32[]{:S(2)}) copy-start(pred[256,512]{0,1:T(8,128)(4,1)} %broadcast_compare_fusion) | copy-start | bytes 393220
  46.1 8.0 copy-start.15
  61.5 117.4 %reduce-scatter.6.cloned.1.call-start = ((), (), s32[]{:S(2)}) async-start(), calls=%async_computation.6 | async-start | bytes 2949120 | tf_op jit(solution)/shard_map/reduce_scatter | solution.py:176
  67.8 4.6 copy-start.13
  67.8 4.6 copy-start.71
  77.7 13.7 %copy-start.59 = (bf16[1024,16]{0,1:T(8,128)(2,1)S(1)}, bf16[1024,16]{0,1:T(8,128)(2,1)}, u32[]{:S(2)}) copy-start(bf16[1024,16]{0,1:T(8,128)(2,1)} %param.23) | copy-start | bytes 98308
  91.4 2.9 copy-start.18
  94.3 2.7 copy-start.56
  99.6 2.9 copy-start.88
  102.5 3.8 copy-start.87
  106.3 10.5 %copy-start.78 = (bf16[1024,512]{0,1:T(8,128)(2,1)}, bf16[1024,512]{0,1:T(8,128)(2,1)S(1)}, u32[]{:S(2)}) copy-start(bf16[1024,512]{0,1:T(8,128)(2,1)S(1)} %get-tuple-element.45) | copy-start | bytes 3145732
  106.3 2.7 copy-start.86
  108.9 9.1 copy-start.79
  109.0 10.4 %copy-start.76 = (bf16[1024,512]{0,1:T(8,128)(2,1)}, bf16[1024,512]{0,1:T(8,128)(2,1)S(1)}, u32[]{:S(2)}) copy-start(bf16[1024,512]{0,1:T(8,128)(2,1)S(1)} %get-tuple-element.53) | copy-start | bytes 3145732
  109.0 37.1 %copy-start.24 = (bf16[1024,512]{0,1:T(8,128)(2,1)}, bf16[1024,512]{0,1:T(8,128)(2,1)S(1)}, u32[]{:S(2)}) copy-start(bf16[1024,512]{0,1:T(8,128)(2,1)S(1)} %get-tuple-element.54) | copy-start | bytes 3145732
  109.0 3.5 copy-start.85
  112.5 8.1 copy-start.81
  112.5 11.4 %copy-start.73 = (bf16[1024,512]{0,1:T(8,128)(2,1)}, bf16[1024,512]{0,1:T(8,128)(2,1)S(1)}, u32[]{:S(2)}) copy-start(bf16[1024,512]{0,1:T(8,128)(2,1)S(1)} %get-tuple-element.51) | copy-start | bytes 3145732
  116.0 11.2 %copy-start.83 = (bf16[1024,512]{0,1:T(8,128)(2,1)}, bf16[1024,512]{0,1:T(8,128)(2,1)S(1)}, u32[]{:S(2)}) copy-start(bf16[1024,512]{0,1:T(8,128)(2,1)S(1)} %get-tuple-element.39) | copy-start | bytes 3145732
  116.0 14.7 %copy-start.74 = (bf16[1024,512]{0,1:T(8,128)(2,1)}, bf16[1024,512]{0,1:T(8,128)(2,1)S(1)}, u32[]{:S(2)}) copy-start(bf16[1024,512]{0,1:T(8,128)(2,1)S(1)} %get-tuple-element.49) | copy-start | bytes 3145732
  146.0 67.4 %reduce-scatter.4.cloned.1.call-start = ((), (), s32[]{:S(2)}) async-start(), calls=%async_computation.5 | async-start | bytes 2621440 | tf_op jit(solution)/shard_map/reduce_scatter | solution.py:177
  146.1 2.7 copy-start.14
  146.1 2.8 copy-start.28
  154.7 102.0 %reduce-scatter.8.cloned.1.call-start = ((), (), s32[]{:S(2)}) async-start(), calls=%async_computation.7 | async-start | bytes 1572864 | tf_op jit(solution)/shard_map/reduce_scatter | solution.py:206
  156.7 4.3 copy-start.19
  156.7 4.3 copy-start.80
  165.6 14.4 %copy-start.58 = (f32[1024,16]{0,1:T(8,128)S(1)}, f32[1024,16]{0,1:T(8,128)}, u32[]{:S(2)}) copy-start(f32[1024,16]{0,1:T(8,128)} %copy-done.57) | copy-start | bytes 196612
  165.6 15.4 %copy-start.9 = (f32[256,1024]{0,1:T(8,128)S(1)}, f32[256,1024]{0,1:T(8,128)}, u32[]{:S(2)}) copy-start(f32[256,1024]{0,1:T(8,128)} %copy-done.8) | copy-start | bytes 3145732
  165.6 15.4 %copy-start.60 = (bf16[1024,16]{0,1:T(8,128)(2,1)S(1)}, bf16[1024,16]{0,1:T(8,128)(2,1)}, u32[]{:S(2)}) copy-start(bf16[1024,16]{0,1:T(8,128)(2,1)} %param.23) | copy-start | bytes 98308
  218.9 4.9 copy-start.54
  228.6 4.5 copy-start.44
  228.6 4.5 copy-start.45
  236.3 184.9 %all-reduce.9.cloned.1.call-start = ((), (), s32[]{:S(2)}) async-start(), calls=%async_computation.10 | async-start | bytes 12582912 | tf_op jit(solution)/shard_map/psum | solution.py:240
  236.8 4.0 copy-start.20
  236.8 4.0 copy-start.77
  240.8 2.4 copy-start.2
  240.8 2.8 copy-start.16
  244.7 3.0 copy-start.6
  244.7 3.0 copy-start.50
  260.9 565.3 %all-reduce.11.cloned.1.call-start = ((), (), s32[]{:S(2)}) async-start(), calls=%async_computation.11 | async-start | bytes 25165824 | tf_op jit(solution)/shard_map/psum | solution.py:181
  260.9 3.3 copy-start.21
  260.9 3.3 copy-start.75
  271.4 2.5 copy-start.35
  271.4 2.5 copy-start.36
  271.4 3.4 copy-start.37
  271.4 3.7 copy-start.38
  271.4 4.1 copy-start.41
  271.4 4.4 copy-start.42
  279.6 672.0 %all-reduce.7.cloned.1.call-start = ((), (), s32[]{:S(2)}) async-start(), calls=%async_computation.8 | async-start | bytes 131072 | tf_op jit(solution)/shard_map/psum | solution.py:244
  421.1 4.2 copy-start.40
  826.2 6.9 copy-start.12
  833.1 4.6 copy-start.11
  (34 other events, 50.8 us)
Sparse Core Ops, SparseCore 0:
  18.3 23.4 all-gather.5
  43.3 22.9 all-gather.9
  68.5 22.8 all-gather.7
  146.2 32.6 reduce-scatter.5
  181.9 31.4 reduce-scatter.3
  236.4 20.3 reduce-scatter.7
  264.4 156.7 all-reduce.8
  426.4 399.7 all-reduce.10
  833.3 118.3 all-reduce.6
where the time goes:
time: 967 us; the launch traced here: 960 us
  waiting for transfers between devices  669 us (69%)
  matrix products  145 us (15%)
  other arithmetic  52.2 us (5%)
  blocking collectives  45.6 us (5%)
  local copies, waits for them, and re-layouts  31.9 us (3%)
  between operations  15.1 us (2%)
    psum x1, waiting for transfers between devices, body(): lax.psum(jnp.stack(g), ('context', 'dp')).astype(F32)  394 us
    psum x1, waiting for transfers between devices, body(): lax.psum((grad_gain_one, grad_gain_two, grad_router_w), everywhere)  110 us
    psum x1, waiting for transfers between devices, body(): lax.psum(tuple((g.astype(BF16) for g in (grad_query_w, grad_key_w, grad_v...  90.1 us
    dot_general x17, matrix products, dot_t(): lax.dot_general(a, b, (((1,), (1,)), ((), ())), preferred_element_type=F32)  47.2 us
    psum x1, blocking collectives, body(): lax.psum((grad_gain_one, grad_gain_two, grad_router_w), everywhere)  39.5 us
    dot_general x17, matrix products, dot(): return jnp.dot(a, b, preferred_element_type=F32)  37.3 us
    dot_general x17, matrix products, t_dot(): lax.dot_general(a, b, (((0,), (0,)), ((), ())), preferred_element_type=F32)  35.9 us
    reduce_scatter x1, waiting for transfers between devices, body(): lax.psum_scatter(partial_y.astype(BF16), 'expert', scatter_dimension=0, t...  30.9 us
  transfers between devices with their start and end apart: 9, of which 8 were waited for; matrix products, arithmetic and copies ran while one was open for 13% of the time, Pallas kernels for 0%

commit v1 on v0

--- a/solution.py
+++ b/solution.py
@@ -178,7 +178,8 @@
         partial_y.astype(BF16), "expert", scatter_dimension=0, tiled=True
     ).astype(F32)
     total_gate, total_up, total_down = (
-        lax.psum(jnp.stack(g), ("context", "dp")).astype(F32) for g in (g_gate, g_up, g_down)
+        jnp.sum(jax.lax.all_gather(jnp.stack(g), axis_name=("context", "dp")), axis=0).astype(F32)
+        for g in (g_gate, g_up, g_down)
     )
     outputs = (y_one + y_two).astype(BF16)[None]
     grad_final = cotangent[0].astype(F32)

time: 967 us -> 2490 us (2.57)
  waiting for transfers between devices: 669 us -> 2140 us
  other arithmetic: 52.2 us -> 102 us
    all_gather x0 -> x3, waiting for transfers between devices: none -> 1870 us  [body(): jax.lax.all_gather(jnp.stack(g), axis_name=('context', 'dp'))]
    psum x1 -> x0, waiting for transfers between devices: 394 us -> none  [body(): lax.psum(jnp.stack(g), ('context', 'dp')).astype(F32)]
    reduce_sum x0 -> x3, other arithmetic: none -> 43.5 us  [body(): jnp.sum(jax.lax.all_gather(jnp.stack(g), axis_name=('context', 'dp')), ax...]
  transfers between devices with their start and end apart: 9 -> 11, of which waited for: 8 -> 10; matrix products, arithmetic and copies ran while one was open for 13% -> 7% of each run, Pallas kernels for 0% -> 0%
where the time goes in v1:
time: 2490 us; the launch traced here: 2480 us
  waiting for transfers between devices  2140 us (86%)
  matrix products  146 us (6%)
  other arithmetic  102 us (4%)
  blocking collectives  45.8 us (2%)
  local copies, waits for them, and re-layouts  28.5 us (1%)
    all_gather x3, waiting for transfers between devices, body(): jax.lax.all_gather(jnp.stack(g), axis_name=('context', 'dp'))  1870 us
    psum x1, waiting for transfers between devices, body(): lax.psum((grad_gain_one, grad_gain_two, grad_router_w), everywhere)  106 us
    psum x1, waiting for transfers between devices, body(): lax.psum(tuple((g.astype(BF16) for g in (grad_query_w, grad_key_w, grad_v...  79.8 us
    dot_general x17, matrix products, dot_t(): lax.dot_general(a, b, (((1,), (1,)), ((), ())), preferred_element_type=F32)  52 us
  transfers between devices with their start and end apart: 11, of which 10 were waited for; matrix products, arithmetic and copies ran while one was open for 7% of the time, Pallas kernels for 0%

profile of v1, /device:TPU:1, one launch (start us, length us, event | category | flops | bytes accessed | tf_op | source)
XLA Modules:
  0.0 2482.8 jit_solution(3626096376444910435)
XLA Ops:
  9.5 2.3 copy.117
  11.8 2.8 convolution_convert_fusion.13
  16.3 1.8 pad_maximum_fusion.4
  19.0 3.9 copy.122
  23.0 2.4 fusion.161
  27.1 14.6 all-gather.12.cloned.1.call-done
  41.7 2.1 fusion.202
  46.0 7.3 fusion.203
  53.3 4.4 fusion.74
  60.9 6.1 all-gather
  67.1 4.6 fusion.16
  71.8 2.6 fusion.18
  74.4 2.6 fusion.20
  77.0 2.6 fusion.22
  79.6 11.8 all-gather.14.cloned.1.call-done
  91.4 2.1 fusion.204
  93.7 2.7 fusion.94
  101.9 3.4 multiply_convert_fusion.1
  105.4 3.6 multiply_convert_fusion.3
  109.0 3.4 multiply_convert_fusion.5
  112.4 3.4 multiply_convert_fusion.7
  118.5 3.3 fusion.103
  121.8 3.3 fusion.118
  125.0 3.3 fusion.114
  128.3 3.5 fusion.129
  131.8 3.2 fusion.125
  135.0 9.9 add_convert_fusion
  144.9 4.6 maximum_maximum_fusion
  149.7 3.0 fusion.101
  155.5 3.1 add_convert_fusion.1
  159.1 2.1 copy.130
  161.1 21.3 reduce-scatter.6.cloned.1.call-done
  184.6 3.3 multiply_reduce_fusion.4
  187.8 29.1 %reduce-scatter.4.cloned.1.call-done = bf16[256,1024]{0,1:T(8,128)(2,1)} async-done(((bf16[1024,1024]{0,1:T(8,128)(2,1)}), bf16[256,1024]{0,1:T(8,128)(2,1)}) %reduce-scatter.4.cloned.1.call-update) | async-done | bytes 524304 | tf_op jit(solution)/shard_map/reduce_scatter | solution.py:177
  217.0 3.0 convert_add_fusion
  223.7 4.9 fusion.1
  228.6 4.8 fusion.78
  233.4 4.5 fusion.3
  241.1 3.0 convolution_multiply_fusion
  244.3 2.1 convolution_convert_fusion.1
  246.3 2.1 convolution_convert_fusion
  248.4 13.1 reduce-scatter.8.cloned.1.call-done
  265.8 3.3 fusion.47
  273.0 2.3 pad_maximum_fusion
  276.9 3.0 fusion.51
  283.8 2.3 pad_maximum_fusion.1
  286.4 3.4 fusion.52
  293.7 2.3 pad_maximum_fusion.2
  299.7 3.4 fusion.206
  303.2 1.8 convolution_add_fusion.2
  306.9 39.7 %all-reduce = (f32[1024]{0:T(1024)}, f32[1024]{0:T(1024)}) all-reduce(f32[1024]{0:T(1024)S(1)} %get-tuple-element.26, f32[1024]{0:T(1024)S(1)} %copy-done.41), channel_id=1, replica_groups=mesh['expert'=4,'context'=2,'dp'=4] {'expert','context','dp'}, use_global_device_ids=true, to_apply=%region_21.22 | all-reduce | flops 2048 | bytes 16384 | tf_op jit(solution)/shard_map/psum | solution.py:245
  346.5 79.8 %all-reduce.7.cloned.1.call-done = (bf16[1024,1024]{1,0:T(8,128)(2,1)}, bf16[1024,512]{1,0:T(8,128)(2,1)}, bf16[1024,512]{1,0:T(8,128)(2,1)}, bf16[1024,1024]{1,0:T(8,128)(2,1)}) async-done(((bf16[1024,1024]{1,0:T(8,128)(2,1)}, bf16[1024,512]{1,0:T(8,128)(2,1)}, bf16[1024,512]{1,0:T(8,128)(2,1)}, bf16[1024,1024]{1,0:T(8,128)(2,1)}), (bf16[1024,1024]{1,0:T(8,128)(2,1)}, bf16[1024,512]{1,0:T(8,128)(2,1)}, ...) | async-done | bytes 6291472 | tf_op jit(solution)/shard_map/psum | solution.py:241
  426.4 4.2 convert_element_type.286
  434.5 2.5 convert_element_type.292
  437.0 629.4 %all-gather.18.cloned.1.call-done = bf16[32,1024,512]{2,1,0:T(8,128)(2,1)} async-done(((bf16[4,1024,512]{2,1,0:T(8,128)(2,1)}), bf16[32,1024,512]{2,1,0:T(8,128)(2,1)}) %all-gather.18.cloned.1.call-update) | async-done | bytes 33554448 | tf_op jit(solution)/shard_map/all_gather | solution.py:181
  1066.4 14.5 reduce_sum.196
  1081.0 6.8 convert_element_type.297
  1087.7 619.7 %all-gather.20.cloned.1.call-done = bf16[32,1024,512]{2,1,0:T(8,128)(2,1)} async-done(((bf16[4,1024,512]{2,1,0:T(8,128)(2,1)}), bf16[32,1024,512]{2,1,0:T(8,128)(2,1)}) %all-gather.20.cloned.1.call-update) | async-done | bytes 33554448 | tf_op jit(solution)/shard_map/all_gather | solution.py:181
  1707.5 14.8 reduce_sum.197
  1722.2 6.8 convert_element_type.302
  1729.0 618.8 %all-gather.22.cloned.1.call-done = bf16[32,512,1024]{2,1,0:T(8,128)(2,1)} async-done(((bf16[4,512,1024]{2,1,0:T(8,128)(2,1)}), bf16[32,512,1024]{2,1,0:T(8,128)(2,1)}) %all-gather.22.cloned.1.call-update) | async-done | bytes 33554448 | tf_op jit(solution)/shard_map/all_gather | solution.py:181
  2347.8 14.2 reduce_sum.198
  2362.0 6.8 convert_element_type.307
  2368.8 105.7 %all-reduce.5.cloned.1.call-done = f32[1024,16]{0,1:T(8,128)} async-done(((f32[1024,16]{0,1:T(8,128)}), f32[1024,16]{0,1:T(8,128)}) %all-reduce.5.cloned.1.call-update) | async-done | bytes 65552 | tf_op jit(solution)/shard_map/psum | solution.py:245
  (230 shorter events, 61.3 us)
Async XLA Ops:
  7.2 50.6 %copy-start = (bf16[1024,1024]{1,0:T(8,128)(2,1)S(1)}, bf16[1024,1024]{1,0:T(8,128)(2,1)}, u32[]{:S(2)}) copy-start(bf16[1024,1024]{1,0:T(8,128)(2,1)} %param.21) | copy-start | bytes 6291460
  7.2 34.5 %all-gather.12.cloned.1.call-start = ((), (), s32[]{:S(2)}) async-start(), calls=%async_computation.3 | async-start | bytes 1572864 | tf_op jit(solution)/shard_map/all_gather | solution.py:103
  11.8 2.8 copy-start.28
  11.8 3.4 copy-start.46
  18.1 49.0 %all-gather.16.cloned.1.call-start = ((), (), s32[]{:S(2)}) async-start(), calls=%async_computation.9 | async-start | bytes 2621440 | tf_op jit(solution)/shard_map/all_gather | solution.py:88
  18.9 72.5 %all-gather.14.cloned.1.call-start = ((), (), s32[]{:S(2)}) async-start(), calls=%async_computation.4 | async-start | bytes 2621440 | tf_op jit(solution)/shard_map/all_gather | solution.py:128
  23.0 2.4 copy-start.45
  53.3 4.5 copy-start.37
  58.8 2.1 copy-start.44
  58.8 8.2 copy-start.39
  60.7 121.6 %reduce-scatter.6.cloned.1.call-start = ((), (), s32[]{:S(2)}) async-start(), calls=%async_computation.6 | async-start | bytes 2949120 | tf_op jit(solution)/shard_map/reduce_scatter | solution.py:176
  67.1 4.6 copy-start.8
  67.1 4.6 copy-start.48
  77.0 14.4 copy-start.35
  91.4 2.3 copy-start.12
  93.7 2.7 copy-start.34
  99.0 2.2 copy-start.47
  99.1 2.9 copy-start.66
  101.9 3.4 copy-start.65
  105.3 10.6 copy-start.56
  105.3 29.7 %copy-start.23 = (bf16[1024,512]{0,1:T(8,128)(2,1)}, bf16[1024,512]{0,1:T(8,128)(2,1)S(1)}, u32[]{:S(2)}) copy-start(bf16[1024,512]{0,1:T(8,128)(2,1)S(1)} %get-tuple-element.44) | copy-start | bytes 3145732
  105.4 3.6 copy-start.64
  109.0 8.2 copy-start.57
  109.0 9.5 copy-start.50
  109.0 3.5 copy-start.63
  112.4 9.3 copy-start.59
  112.4 12.6 copy-start.52
  115.9 12.4 copy-start.61
  115.9 15.9 copy-start.54
  149.6 67.4 %reduce-scatter.4.cloned.1.call-start = ((), (), s32[]{:S(2)}) async-start(), calls=%async_computation.5 | async-start | bytes 2621440 | tf_op jit(solution)/shard_map/reduce_scatter | solution.py:177
  149.6 3.0 copy-start.9
  149.6 3.1 copy-start.18
  158.6 26.0 %copy-start.36 = (bf16[1024,16]{0,1:T(8,128)(2,1)S(1)}, bf16[1024,16]{0,1:T(8,128)(2,1)}, u32[]{:S(2)}) copy-start(bf16[1024,16]{0,1:T(8,128)(2,1)} %param.23) | copy-start | bytes 98308
  158.6 26.0 %copy-start.40 = (f32[256]{0:T(256)S(1)}, f32[256]{0:T(256)}, u32[]{:S(2)}) copy-start(f32[256]{0:T(256)} %copy-done.39) | copy-start | bytes 3076
  158.6 102.9 %reduce-scatter.8.cloned.1.call-start = ((), (), s32[]{:S(2)}) async-start(), calls=%async_computation.7 | async-start | bytes 1572864 | tf_op jit(solution)/shard_map/reduce_scatter | solution.py:207
  184.6 3.3 copy-start.42
  220.9 2.8 copy-start.38
  233.4 4.5 copy-start.27
  237.9 2.0 copy-start.2
  241.0 3.0 copy-start.33
  241.0 185.4 %all-reduce.7.cloned.1.call-start = ((), (), s32[]{:S(2)}) async-start(), calls=%async_computation.13 | async-start | bytes 12582912 | tf_op jit(solution)/shard_map/psum | solution.py:241
  244.2 2.1 copy-start.4
  244.2 2.1 copy-start.30
  262.4 1.6 copy-start.31
  265.5 800.9 %all-gather.18.cloned.1.call-start = ((), (), s32[]{:S(2)}) async-start(), calls=%async_computation.10 | async-start | bytes 37748736 | tf_op jit(solution)/shard_map/all_gather | solution.py:181
  265.8 3.3 copy-start.13
  265.8 3.3 copy-start.58
  275.3 1.5 copy-start.24
  275.3 1432.1 %all-gather.20.cloned.1.call-start = ((), (), s32[]{:S(2)}) async-start(), calls=%async_computation.11 | async-start | bytes 37748736 | tf_op jit(solution)/shard_map/all_gather | solution.py:181
  276.9 3.0 copy-start.14
  276.9 3.0 copy-start.51
  286.1 3.7 copy-start.15
  286.2 2061.7 %all-gather.22.cloned.1.call-start = ((), (), s32[]{:S(2)}) async-start(), calls=%async_computation.12 | async-start | bytes 37748736 | tf_op jit(solution)/shard_map/all_gather | solution.py:181
  286.4 3.4 copy-start.49
  296.0 2.1 copy-start.6
  296.0 2.1 copy-start.43
  296.1 2178.4 %all-reduce.5.cloned.1.call-start = ((), (), s32[]{:S(2)}) async-start(), calls=%async_computation.8 | async-start | bytes 131072 | tf_op jit(solution)/shard_map/psum | solution.py:245
  299.7 3.5 copy-start.7
  303.2 1.8 copy-start.32
  303.2 1.8 copy-start.21
  426.4 4.2 copy-start.26
  430.5 1.6 copy-start.25
  432.1 2.3 copy-start.10
  2362.0 114.0 %copy-start.1 = (bf16[1024,1024]{1,0:T(8,128)(2,1)S(1)}, bf16[1024,1024]{1,0:T(8,128)(2,1)}, u32[]{:S(2)}) copy-start(bf16[1024,1024]{1,0:T(8,128)(2,1)} %param.21) | copy-start | bytes 6291460
  (14 other events, 16.8 us)
Sparse Core Ops, SparseCore 0:
  18.3 23.4 all-gather.11
  43.3 22.9 all-gather.15
  68.4 22.9 all-gather.13
  149.7 32.6 reduce-scatter.5
  185.5 31.4 reduce-scatter.3
  241.1 20.3 reduce-scatter.7
  269.7 156.6 all-reduce.6
  428.5 637.8 all-gather.17
  1068.5 638.9 all-gather.19
  1708.9 638.9 all-gather.21
  2354.0 120.4 all-reduce.4
